TPU v7x, 128 devices: a whole 4x4x4 slice. The times are simulated.
128 devices in a mesh: section: 2 (over core), shard: 16 (over y, z), replica: 4 (over x).
Axes of the slice: x: 4, y: 4, z: 4, core: 2. Of those that a mesh axis runs over, the one named last changes fastest.
Arguments:
- tokens: bfloat16 [8, 1024, 768], P('replica', 'shard'), may hold values from -6 to 6
- cotangent: bfloat16 [8, 1024, 768], P('replica', 'shard'), may hold values from -6 to 6
- query_key_value_weight: bfloat16 [2, 768, 2304], P('section', 'shard'), may hold values from -0.21875 to 0.21875
- attention_output_weight: bfloat16 [2, 768, 768], P('section', 'shard'), may hold values from -0.875 to 0.875
- gain_attn: bfloat16 [2, 768], P('section', 'shard'), may hold values from 0.5 to 1.5
- gain_ffn: bfloat16 [2, 768], P('section', 'shard'), may hold values from 0.5 to 1.5
- rel_table: bfloat16 [2, 32, 12], P('section', 'shard'), may hold values from -4 to 4
- w_in: bfloat16 [2, 64, 768, 3072], P('section', ('shard', 'replica')), may hold values from -0.21875 to 0.21875
- w_out_exp: bfloat16 [2, 64, 3072, 768], P('section', ('shard', 'replica')), may hold values from -0.109375 to 0.109375
- expert_ids: int32 [2, 8, 1024, 2], P('section', 'replica', 'shard'), may hold values from 0 to 63, all different within a row; in each aligned block of 64 rows (0 to 63, 64 to 127, ..., all dimensions but the last counted through in order) at most 3 rows name the same one
- gates: float32 [2, 8, 1024, 2], P('section', 'replica', 'shard'), may hold values from 0.2 to 0.8
- seg_ids: int32 [8, 1024], P('replica'), may hold values from 0 to 3, as said below
- buckets: int32 [1024], replicated, may hold values from 0 to 31, as said below
Outputs:
- activations: bfloat16 [2, 8, 1024, 768], P('section', 'replica', 'shard')
- section_grads: bfloat16 [2, 8, 1024, 768], P('section', 'replica', 'shard')
- grad_qkv: bfloat16 [2, 768, 2304], P('section', 'shard')
- grad_attn_out: bfloat16 [2, 768, 768], P('section', 'shard')
- grad_gain_attn: bfloat16 [2, 768], P('section', 'shard')
- grad_gain_ffn: bfloat16 [2, 768], P('section', 'shard')
- grad_table: bfloat16 [2, 32, 12], P('section', 'shard')
- grad_w_in: bfloat16 [2, 64, 768, 3072], P('section', ('shard', 'replica'))
- grad_w_out_exp: bfloat16 [2, 64, 3072, 768], P('section', ('shard', 'replica'))
Inputs may be any that keep to these rules, and one draw needn't show every extreme that they name: `seg_ids`: within a sequence the document number starts at 0 and never falls; of the 2 sequences of each replica group one is a single document. The bucket of distance 0 is 0, buckets never fall as the distance grows, and every bucket occurs. `expert_ids`: each token names two different experts; within each aligned block of 64 tokens of a sequence no expert is named more than 3 times.
All inputs are finite; a program needn't handle non-finite values.
Results may differ from a plain program's by a relative error of at most 0.028.
Values may be sent and summed in bfloat16 or wider, within the bound.
A program may use at most 192 MiB of HBM per device.

v0:
```python
import jax
import jax.numpy as jnp
from jax import lax
from jax.sharding import PartitionSpec as P

peak_score = lax.Precision.HIGHEST


def shifted(array, axis, by):
    length = lax.axis_size(axis)
    pairs = [(i, i + by) for i in range(length) if 0 <= i + by < length]
    return lax.ppermute(array, axis, pairs)


def norm_piece(inputs, gain_vec):
    return inputs * lax.rsqrt(jnp.mean(inputs * inputs, axis=-1, keepdims=True) + 1e-06) * gain_vec


def bucket_onehot(starts, limits, query_pos, key_pos):
    distance = jnp.maximum(query_pos[:, None] - key_pos[None, :], 0)
    above = distance[None] >= starts[:, None, None]
    below = distance[None] < limits[:, None, None]
    return (above & below).astype(jnp.float32)


def attn_logits(queries, keys_all, position_bias_lookup, indicator_matrix, allowed):
    raw_scores = (
        jnp.einsum("qhd,khd->hqk", queries, keys_all, preferred_element_type=jnp.float32) * 0.125
    )
    relative_position_bias = jnp.einsum(
        "nlz,nf->flz", indicator_matrix, position_bias_lookup, precision=peak_score
    )
    return jnp.where(allowed[None], raw_scores + relative_position_bias, -1e30)


def body(
    tokens,
    cotangent,
    query_key_value_weight,
    attention_output_weight,
    gain_attn,
    gain_ffn,
    rel_table,
    w_in,
    w_out_exp,
    expert_ids,
    gates,
    seg_ids,
    buckets,
):
    micro_count = tokens.shape[0]
    row_count = tokens.shape[1]
    model_width = tokens.shape[2]
    seq_length = seg_ids.shape[1]
    is_first = lax.axis_index("section") == 0
    shard_pos = lax.axis_index("shard")
    gathered = (
        lax.all_gather(query_key_value_weight[0], "shard", axis=0, tiled=True),
        lax.all_gather(attention_output_weight[0], "shard", axis=0, tiled=True),
        lax.all_gather(gain_attn[0], "shard", axis=0, tiled=True),
        lax.all_gather(gain_ffn[0], "shard", axis=0, tiled=True),
        lax.all_gather(rel_table[0], "shard", axis=0, tiled=True),
    )
    wqkv_full, wout_full, gain_one_bf, gain_two_bf, table_bf = gathered
    gain_one = gain_one_bf.astype(jnp.float32)
    gain_two = gain_two_bf.astype(jnp.float32)
    position_bias_lookup = table_bf.astype(jnp.float32)
    bucket_count, head_count = position_bias_lookup.shape
    head_dim = model_width // head_count
    expert_in = w_in[0, 0]
    expert_out = w_out_exp[0, 0]
    expert_count = lax.axis_size(("shard", "replica"))
    capacity = max(2, 3 * row_count // expert_count)
    bucket_range = jnp.arange(bucket_count)
    starts = jnp.sum((buckets[None, :] < bucket_range[:, None]).astype(jnp.int32), axis=1)
    limits = jnp.concatenate([starts[1:], jnp.full((1,), seq_length, jnp.int32)])
    query_pos = shard_pos * row_count + jnp.arange(row_count)
    key_pos = jnp.arange(seq_length)
    local_indicator_matrix = bucket_onehot(starts, limits, query_pos, key_pos)
    four_shape = (row_count, head_count, head_dim)
    full_shape = (seq_length, head_count, head_dim)
    kept_states = []
    passed_outs = []
    received = jnp.zeros((row_count, model_width), jnp.bfloat16)
    for step_index in range(micro_count + 1):
        early = min(step_index, micro_count - 1)
        late = max(step_index - 1, 0)
        layer_in = jnp.where(is_first, tokens[early], received).astype(jnp.float32)
        seg_now = jnp.where(is_first, seg_ids[early], seg_ids[late])
        ids_now = jnp.where(is_first, expert_ids[0, early], expert_ids[0, late])
        gate_now = jnp.where(is_first, gates[0, early], gates[0, late])
        normalized_input = norm_piece(layer_in, gain_one).astype(jnp.bfloat16)
        query_key_value = jnp.dot(
            normalized_input, wqkv_full, preferred_element_type=jnp.float32
        ).astype(jnp.bfloat16)
        queries = query_key_value[:, :model_width].reshape(four_shape)
        kv_all = lax.all_gather(query_key_value[:, model_width:], "shard", axis=0, tiled=True)
        keys_all = kv_all[:, :model_width].reshape(full_shape)
        values_all = kv_all[:, model_width:].reshape(full_shape)
        seg_own = lax.dynamic_slice_in_dim(seg_now, shard_pos * row_count, row_count)
        allowed = (key_pos[None, :] <= query_pos[:, None]) & (seg_own[:, None] == seg_now[None, :])
        logits = attn_logits(
            queries, keys_all, position_bias_lookup, local_indicator_matrix, allowed
        )
        row_max = jnp.max(logits, axis=-1, keepdims=True)
        row_exp = jnp.exp(logits - row_max)
        row_total = jnp.sum(row_exp, axis=-1, keepdims=True)
        log_total = row_max + jnp.log(row_total)
        attn_probs = row_exp / row_total
        mixed_heads_output = jnp.einsum(
            "hqk,khd->qhd",
            attn_probs.astype(jnp.bfloat16),
            values_all,
            preferred_element_type=jnp.float32,
        )
        mixed_heads_output = mixed_heads_output.astype(jnp.bfloat16).reshape(row_count, model_width)
        hidden = layer_in + jnp.dot(
            mixed_heads_output, wout_full, preferred_element_type=jnp.float32
        )
        normed_two = norm_piece(hidden, gain_two).astype(jnp.bfloat16)
        flat_ids = ids_now.reshape(-1)
        hits = (flat_ids[:, None] == jnp.arange(expert_count)[None, :]).astype(jnp.int32)
        slot_rank = jnp.sum((jnp.cumsum(hits, axis=0) - 1) * hits, axis=1)
        slot_index = flat_ids * capacity + slot_rank
        slot_hits = (slot_index[None, :] == jnp.arange(expert_count * capacity)[:, None]).astype(
            jnp.float32
        )
        placed = slot_hits.reshape(expert_count * capacity, row_count, 2)
        scatter_mat = jnp.sum(placed, axis=2)
        gate_mat = jnp.sum(placed * gate_now[None], axis=2)
        outgoing = jnp.dot(
            scatter_mat.astype(jnp.bfloat16), normed_two, preferred_element_type=jnp.float32
        )
        outgoing = outgoing.astype(jnp.bfloat16).reshape(expert_count, capacity, model_width)
        arrived = lax.all_to_all(
            outgoing, ("shard", "replica"), split_axis=0, concat_axis=0, tiled=True
        )
        slot_span = arrived.shape[1]
        flat_rows = arrived.reshape(-1, model_width)
        pre_act = jnp.dot(flat_rows, expert_in, preferred_element_type=jnp.float32)
        expert_gelu_out = jax.nn.gelu(pre_act).astype(jnp.bfloat16)
        result = jnp.dot(expert_gelu_out, expert_out, preferred_element_type=jnp.float32).astype(
            jnp.bfloat16
        )
        result = result.reshape(expert_count, slot_span, model_width)
        returned = lax.all_to_all(
            result, ("shard", "replica"), split_axis=0, concat_axis=0, tiled=True
        )
        returned, expert_rows, pre_act = (
            returned,
            arrived,
            pre_act.reshape(expert_count, slot_span, -1),
        )
        expert_sum = jnp.dot(
            gate_mat.T, returned.reshape(-1, model_width).astype(jnp.float32), precision=peak_score
        )
        layer_out = (hidden + expert_sum).astype(jnp.bfloat16)
        passed_outs.append(layer_out)
        received = shifted(layer_out, "section", 1)
        kept_states.append(
            (
                layer_in,
                normalized_input,
                query_key_value,
                kv_all,
                seg_now,
                seg_own,
                allowed,
                log_total,
                mixed_heads_output,
                hidden,
                scatter_mat,
                gate_mat,
                expert_rows,
                pre_act,
            )
        )
    ff_width = expert_in.shape[1]
    grad_qkv = jnp.zeros(wqkv_full.shape, jnp.float32)
    grad_out = jnp.zeros(wout_full.shape, jnp.float32)
    grad_one = jnp.zeros((model_width,), jnp.float32)
    grad_two = jnp.zeros((model_width,), jnp.float32)
    grad_bias = jnp.zeros(position_bias_lookup.shape, jnp.float32)
    grad_in = jnp.zeros(expert_in.shape, jnp.float32)
    grad_eout = jnp.zeros(expert_out.shape, jnp.float32)
    coming = jnp.zeros((row_count, model_width), jnp.bfloat16)
    back_outs = []
    for step_index in range(micro_count + 1):
        (
            layer_in,
            normalized_input,
            query_key_value,
            kv_all,
            seg_now,
            seg_own,
            allowed,
            log_total,
            mixed_heads_output,
            hidden,
            scatter_mat,
            gate_mat,
            expert_rows,
            pre_act,
        ) = kept_states[micro_count - step_index]
        if step_index < micro_count:
            last_grad = cotangent[micro_count - 1 - step_index].astype(jnp.float32)
        else:
            last_grad = jnp.zeros((row_count, model_width), jnp.float32)
        grad_now = jnp.where(is_first, coming.astype(jnp.float32), last_grad)
        grad_slots = jnp.dot(gate_mat, grad_now, precision=peak_score).astype(jnp.bfloat16)
        grad_slots = grad_slots.reshape(expert_count, capacity, model_width)
        grad_arrived = lax.all_to_all(
            grad_slots, ("shard", "replica"), split_axis=0, concat_axis=0, tiled=True
        ).reshape(-1, model_width)
        flat_pre = pre_act.reshape(-1, ff_width)
        gelu_out = jax.nn.gelu(flat_pre).astype(jnp.bfloat16)
        grad_eout = grad_eout + jnp.dot(
            gelu_out.T, grad_arrived, preferred_element_type=jnp.float32
        )
        grad_gelu = jnp.dot(grad_arrived, expert_out.T, preferred_element_type=jnp.float32)
        unused_out, gelu_back = jax.vjp(jax.nn.gelu, flat_pre)
        grad_pre = gelu_back(grad_gelu)[0].astype(jnp.bfloat16)
        grad_in = grad_in + jnp.dot(
            expert_rows.reshape(-1, model_width).T, grad_pre, preferred_element_type=jnp.float32
        )
        grad_rows = jnp.dot(grad_pre, expert_in.T, preferred_element_type=jnp.float32).astype(
            jnp.bfloat16
        )
        grad_rows = grad_rows.reshape(expert_count, capacity, model_width)
        grad_back = lax.all_to_all(
            grad_rows, ("shard", "replica"), split_axis=0, concat_axis=0, tiled=True
        ).reshape(-1, model_width)
        grad_normed_two = jnp.dot(
            scatter_mat.T.astype(jnp.bfloat16), grad_back, preferred_element_type=jnp.float32
        )
        unused_two, norm_back_two = jax.vjp(norm_piece, hidden, gain_two)
        grad_hidden_norm, grad_gain_two = norm_back_two(grad_normed_two)
        grad_two = grad_two + grad_gain_two
        grad_hidden = grad_now + grad_hidden_norm
        grad_attn = grad_hidden.astype(jnp.bfloat16)
        grad_out = grad_out + jnp.dot(
            mixed_heads_output.T, grad_attn, preferred_element_type=jnp.float32
        )
        grad_mixed = jnp.dot(grad_attn, wout_full.T, preferred_element_type=jnp.float32).astype(
            jnp.bfloat16
        )
        grad_mixed_heads = grad_mixed.reshape(four_shape)
        queries = query_key_value[:, :model_width].reshape(four_shape)
        keys_all = kv_all[:, :model_width].reshape(full_shape)
        values_all = kv_all[:, model_width:].reshape(full_shape)
        logits = attn_logits(
            queries, keys_all, position_bias_lookup, local_indicator_matrix, allowed
        )
        attn_probs = jnp.exp(logits - log_total)
        grad_probs = jnp.einsum(
            "qhd,khd->hqk", grad_mixed_heads, values_all, preferred_element_type=jnp.float32
        )
        row_delta = jnp.sum(attn_probs * grad_probs, axis=-1, keepdims=True)
        score_gradient = attn_probs * (grad_probs - row_delta)
        grad_bias = grad_bias + jnp.einsum(
            "zxo,gxo->gz", score_gradient, local_indicator_matrix, precision=peak_score
        )
        scores_low = score_gradient.astype(jnp.bfloat16)
        grad_query = (
            jnp.einsum("hqk,khd->qhd", scores_low, keys_all, preferred_element_type=jnp.float32)
            * 0.125
        )
        grad_query = grad_query.astype(jnp.bfloat16).reshape(row_count, model_width)
        probs_low = attn_probs.astype(jnp.bfloat16)
        key_grad = (
            jnp.einsum("hqk,qhd->khd", scores_low, queries, preferred_element_type=jnp.float32)
            * 0.125
        )
        value_grad = jnp.einsum(
            "hqk,qhd->khd", probs_low, grad_mixed_heads, preferred_element_type=jnp.float32
        )
        grad_kv = lax.psum_scatter(
            jnp.concatenate(
                [
                    key_grad.reshape(row_count * lax.axis_size("shard"), model_width),
                    value_grad.reshape(row_count * lax.axis_size("shard"), model_width),
                ],
                1,
            ).astype(jnp.bfloat16),
            "shard",
            scatter_dimension=0,
            tiled=True,
        )
        grad_qkv_rows = jnp.concatenate([grad_query, grad_kv], 1)
        grad_qkv = grad_qkv + jnp.dot(
            normalized_input.T, grad_qkv_rows, preferred_element_type=jnp.float32
        )
        grad_normed = jnp.dot(grad_qkv_rows, wqkv_full.T, preferred_element_type=jnp.float32)
        unused_one, norm_back_one = jax.vjp(norm_piece, layer_in, gain_one)
        grad_input_norm, grad_gain_one = norm_back_one(grad_normed)
        grad_one = grad_one + grad_gain_one
        grad_input = (grad_hidden + grad_input_norm).astype(jnp.bfloat16)
        back_outs.append(grad_input)
        coming = shifted(grad_input, "section", -1)
    first_acts = jnp.stack([passed_outs[index] for index in range(micro_count)])
    second_acts = jnp.stack([passed_outs[index + 1] for index in range(micro_count)])
    activations = jnp.where(is_first, first_acts, second_acts)[None]
    first_grads = jnp.stack([back_outs[micro_count - index] for index in range(micro_count)])
    second_grads = jnp.stack([back_outs[micro_count - 1 - index] for index in range(micro_count)])
    section_grads = jnp.where(is_first, first_grads, second_grads)[None]
    shares = (
        lax.psum_scatter(
            grad_qkv.astype(jnp.bfloat16), "shard", scatter_dimension=0, tiled=True
        ).astype(jnp.float32),
        lax.psum_scatter(
            grad_out.astype(jnp.bfloat16), "shard", scatter_dimension=0, tiled=True
        ).astype(jnp.float32),
        lax.psum_scatter(
            grad_one.astype(jnp.bfloat16), "shard", scatter_dimension=0, tiled=True
        ).astype(jnp.float32),
        lax.psum_scatter(
            grad_two.astype(jnp.bfloat16), "shard", scatter_dimension=0, tiled=True
        ).astype(jnp.float32),
        lax.psum_scatter(
            grad_bias.astype(jnp.bfloat16), "shard", scatter_dimension=0, tiled=True
        ).astype(jnp.float32),
    )
    summed = (
        lax.psum(shares[0].astype(jnp.bfloat16), "replica").astype(jnp.float32),
        lax.psum(shares[1].astype(jnp.bfloat16), "replica").astype(jnp.float32),
        lax.psum(shares[2].astype(jnp.bfloat16), "replica").astype(jnp.float32),
        lax.psum(shares[3].astype(jnp.bfloat16), "replica").astype(jnp.float32),
        lax.psum(shares[4].astype(jnp.bfloat16), "replica").astype(jnp.float32),
    )
    return (
        activations,
        section_grads,
        summed[0].astype(jnp.bfloat16)[None],
        summed[1].astype(jnp.bfloat16)[None],
        summed[2].astype(jnp.bfloat16)[None],
        summed[3].astype(jnp.bfloat16)[None],
        summed[4].astype(jnp.bfloat16)[None],
        grad_in.astype(jnp.bfloat16)[None, None],
        grad_eout.astype(jnp.bfloat16)[None, None],
    )


def solution(mesh):
    in_specs = (
        P("replica", "shard", None),
        P("replica", "shard", None),
        P("section", "shard", None),
        P("section", "shard", None),
        P("section", "shard"),
        P("section", "shard"),
        P("section", "shard", None),
        P("section", ("shard", "replica"), None, None),
        P("section", ("shard", "replica"), None, None),
        P("section", "replica", "shard", None),
        P("section", "replica", "shard", None),
        P("replica", None),
        P(),
    )
    out_specs = (
        P("section", "replica", "shard", None),
        P("section", "replica", "shard", None),
        P("section", "shard", None),
        P("section", "shard", None),
        P("section", "shard"),
        P("section", "shard"),
        P("section", "shard", None),
        P("section", ("shard", "replica"), None, None),
        P("section", ("shard", "replica"), None, None),
    )
    return jax.shard_map(body, mesh=mesh, in_specs=in_specs, out_specs=out_specs, check_vma=False)
```

profile of v0, /device:TPU:116, one launch (start us, length us, event | category | flops | bytes accessed | tf_op | source)
XLA Modules:
  0.0 1111.8 jit_solution(10002986047568464344)
XLA Ops:
  11.6 30.4 %all-reduce.6 = (bf16[768]{0:T(1024)(128)(2,1)S(1)}, bf16[768]{0:T(1024)(128)(2,1)S(1)}) all-reduce(bf16[768]{0:T(1024)(128)(2,1)S(1)} %dynamic-update-slice, bf16[768]{0:T(1024)(128)(2,1)S(1)} %dynamic-update-slice.1), channel_id=2, replica_groups=mesh['section'=2,'shard'=16,'replica'=4] {'shard'}, use_global_device_ids=true, to_apply=%add | all-reduce | flops 1536 | bytes 6144
  43.7 14.7 %all-gather.17.cloned.1.call-done = bf16[1,768,2304]{2,1,0:T(8,128)(2,1)} async-done(((bf16[1,48,2304]{2,1,0:T(8,128)(2,1)}), bf16[1,768,2304]{2,1,0:T(8,128)(2,1)}) %all-gather.17.cloned.1.call-update) | async-done | bytes 3538960 | tf_op jit(solution)/shard_map/all_gather | solution.py:58
  67.4 21.5 %all-gather.2 = bf16[1,32,12]{2,0,1:T(2,128)(2,1)S(1)} all-gather(bf16[1,2,12]{2,0,1:T(2,128)(2,1)S(1)} %copy.134), channel_id=4, replica_groups=mesh['section'=2,'shard'=16,'replica'=4] {'shard'}, dimensions={1}, use_global_device_ids=true | all-gather | bytes 816 | tf_op jit(solution)/shard_map/all_gather | solution.py:62
  93.3 15.9 %all-gather.11.cloned.1.call-done = bf16[1024,1536]{1,0:T(8,128)(2,1)} async-done(((bf16[64,1536]{1,0:T(8,128)(2,1)}), bf16[1024,1536]{1,0:T(8,128)(2,1)}) %all-gather.11.cloned.1.call-update) | async-done | bytes 3145744 | tf_op jit(solution)/shard_map/all_gather | solution.py:97
  123.2 30.5 %all-gather.19.cloned.1.call-done = bf16[1,768,768]{2,1,0:T(8,128)(2,1)} async-done(((bf16[1,48,768]{2,1,0:T(8,128)(2,1)}), bf16[1,768,768]{2,1,0:T(8,128)(2,1)}) %all-gather.19.cloned.1.call-update) | async-done | bytes 1179664 | tf_op jit(solution)/shard_map/all_gather | solution.py:59
  157.4 16.1 %all_to_all.60 = bf16[64,3,768]{2,1,0:T(4,128)(2,1)S(1)} all-to-all(bf16[64,3,768]{2,1,0:T(4,128)(2,1)S(1)} %reshape.739), channel_id=1, replica_groups=mesh['section'=2,'shard'=16,'replica'=4] {'shard','replica'}, dimensions={0} | all-to-all | bytes 589824 | tf_op jit(solution)/shard_map/all_to_all | solution.py:135
  185.9 16.7 %all_to_all.61 = bf16[64,3,768]{2,1,0:T(4,128)(2,1)} all-to-all(bf16[64,3,768]{2,1,0:T(4,128)(2,1)} %reshape.741), channel_id=1, replica_groups=mesh['section'=2,'shard'=16,'replica'=4] {'shard','replica'}, dimensions={0} | all-to-all | bytes 589824 | tf_op jit(solution)/shard_map/all_to_all | solution.py:146
  216.1 43.1 %all-gather.13.cloned.1.call-done = bf16[1024,1536]{1,0:T(8,128)(2,1)} async-done(((bf16[64,1536]{1,0:T(8,128)(2,1)}), bf16[1024,1536]{1,0:T(8,128)(2,1)}) %all-gather.13.cloned.1.call-update) | async-done | bytes 3145744 | tf_op jit(solution)/shard_map/all_gather | solution.py:97
  281.9 16.8 %all_to_all.62 = bf16[64,3,768]{2,1,0:T(4,128)(2,1)} all-to-all(bf16[64,3,768]{2,1,0:T(4,128)(2,1)} %reshape.747), channel_id=1, replica_groups=mesh['section'=2,'shard'=16,'replica'=4] {'shard','replica'}, dimensions={0} | all-to-all | bytes 589824 | tf_op jit(solution)/shard_map/all_to_all | solution.py:135
  312.1 16.7 %all_to_all.63 = bf16[64,3,768]{2,1,0:T(4,128)(2,1)} all-to-all(bf16[64,3,768]{2,1,0:T(4,128)(2,1)} %reshape.749), channel_id=1, replica_groups=mesh['section'=2,'shard'=16,'replica'=4] {'shard','replica'}, dimensions={0} | all-to-all | bytes 589824 | tf_op jit(solution)/shard_map/all_to_all | solution.py:146
  342.5 10.9 all-to-all-start.6
  356.7 32.5 %all-gather.15.cloned.1.call-done = bf16[1024,1536]{1,0:T(8,128)(2,1)} async-done(((bf16[64,1536]{1,0:T(8,128)(2,1)}), bf16[1024,1536]{1,0:T(8,128)(2,1)}) %all-gather.15.cloned.1.call-update) | async-done | bytes 3145744 | tf_op jit(solution)/shard_map/all_gather | solution.py:97
  411.6 10.6 all-to-all-start.4
  444.8 10.9 all-to-all-start.7
  489.1 71.6 %reduce-scatter.16.cloned.1.call-done = bf16[64,1536]{1,0:T(8,128)(2,1)} async-done(((bf16[1024,1536]{1,0:T(8,128)(2,1)}), bf16[64,1536]{1,0:T(8,128)(2,1)}) %reduce-scatter.16.cloned.1.call-update) | async-done | bytes 196624
  573.5 17.2 %all_to_all.64 = bf16[64,3,768]{2,1,0:T(4,128)(2,1)} all-to-all(bf16[64,3,768]{2,1,0:T(4,128)(2,1)} %reshape.767), channel_id=1, replica_groups=mesh['section'=2,'shard'=16,'replica'=4] {'shard','replica'}, dimensions={0} | all-to-all | bytes 589824 | tf_op jit(solution)/shard_map/all_to_all | solution.py:212
  605.8 10.9 all-to-all-start.9
  650.0 71.7 %reduce-scatter.18.cloned.1.call-done = bf16[64,1536]{1,0:T(8,128)(2,1)} async-done(((bf16[1024,1536]{1,0:T(8,128)(2,1)}), bf16[64,1536]{1,0:T(8,128)(2,1)}) %reduce-scatter.18.cloned.1.call-update) | async-done | bytes 196624
  734.4 17.2 %all_to_all.65 = bf16[64,3,768]{2,1,0:T(4,128)(2,1)} all-to-all(bf16[64,3,768]{2,1,0:T(4,128)(2,1)} %reshape.775), channel_id=1, replica_groups=mesh['section'=2,'shard'=16,'replica'=4] {'shard','replica'}, dimensions={0} | all-to-all | bytes 589824 | tf_op jit(solution)/shard_map/all_to_all | solution.py:212
  766.8 10.9 all-to-all-start.11
  823.0 59.6 %reduce-scatter.20.cloned.1.call-done = bf16[64,1536]{1,0:T(8,128)(2,1)} async-done(((bf16[1024,1536]{1,0:T(8,128)(2,1)}), bf16[64,1536]{1,0:T(8,128)(2,1)}) %reduce-scatter.20.cloned.1.call-update) | async-done | bytes 196624
  899.9 10.4 all-to-all-start.5
  979.8 64.1 %all-reduce.5 = (bf16[768]{0:T(1024)(128)(2,1)S(1)}, bf16[768]{0:T(1024)(128)(2,1)S(1)}, bf16[32,12]{1,0:T(8,128)(2,1)S(1)}) all-reduce(bf16[768]{0:T(1024)(128)(2,1)S(1)} %add_convert_fusion.5, bf16[768]{0:T(1024)(128)(2,1)S(1)} %add_convert_fusion.4, ...), channel_id=12, replica_groups=mesh['section'=2,'shard'=16,'replica'=4] {'shard'}, use_global_device_ids=true, to_apply=%region_44.45.clone | all-reduce | flops 1920 | bytes 7680
  1056.5 45.5 %all-reduce.11.cloned.1.call-done = (bf16[1,48,2304]{2,1,0:T(8,128)(2,1)}, bf16[1,48,768]{2,1,0:T(8,128)(2,1)}) async-done(((bf16[1,48,2304]{2,1,0:T(8,128)(2,1)}, bf16[1,48,768]{2,1,0:T(8,128)(2,1)}), (bf16[1,48,2304]{2,1,0:T(8,128)(2,1)}, bf16[1,48,768]{2,1,0:T(8,128)(2,1)})) %all-reduce.11.cloned.1.call-update) | async-done | bytes 294928 | tf_op jit(solution)/shard_map/psum | solution.py:324
  (523 shorter events, 427.6 us)
Async XLA Ops:
  7.2 51.2 %all-gather.17.cloned.1.call-start = ((), (), s32[]{:S(2)}) async-start(), calls=%async_computation.22 | async-start | bytes 3760128 | tf_op jit(solution)/shard_map/all_gather | solution.py:58
  7.9 101.2 %all-gather.11.cloned.1.call-start = ((), (), s32[]{:S(2)}) async-start(), calls=%async_computation.17 | async-start | bytes 3342336 | tf_op jit(solution)/shard_map/all_gather | solution.py:97
  62.0 91.8 %all-gather.19.cloned.1.call-start = ((), (), s32[]{:S(2)}) async-start(), calls=%async_computation.23 | async-start | bytes 1253376 | tf_op jit(solution)/shard_map/all_gather | solution.py:59
  62.7 196.5 %all-gather.13.cloned.1.call-start = ((), (), s32[]{:S(2)}) async-start(), calls=%async_computation.18 | async-start | bytes 3342336 | tf_op jit(solution)/shard_map/all_gather | solution.py:97
  205.9 2.2 collective-permute-start
  212.1 177.1 %all-gather.15.cloned.1.call-start = ((), (), s32[]{:S(2)}) async-start(), calls=%async_computation.19 | async-start | bytes 3342336 | tf_op jit(solution)/shard_map/all_gather | solution.py:97
  332.1 2.2 collective-permute-start.1
  342.5 69.1 %all-to-all-start.6 = ((bf16[64,3,768]{2,1,0:T(4,128)(2,1)}), bf16[64,3,768]{2,1,0:T(4,128)(2,1)}, u32[]{:S(2)}, u32[]{:S(2)}) async-start(bf16[64,3,768]{2,1,0:T(4,128)(2,1)} %reshape.759), calls=%async_computation.6 | async-start | bytes 786432 | tf_op jit(solution)/shard_map/all_to_all | solution.py:212
  411.6 16.6 %all-to-all-start.4 = ((bf16[64,3,768]{2,1,0:T(4,128)(2,1)}), bf16[64,3,768]{2,1,0:T(4,128)(2,1)}, u32[]{:S(2)}, u32[]{:S(2)}) async-start(bf16[64,3,768]{2,1,0:T(4,128)(2,1)} %reshape.755), calls=%async_computation.4 | async-start | bytes 786432 | tf_op jit(solution)/shard_map/all_to_all | solution.py:135
  444.8 16.7 %all-to-all-start.7 = ((bf16[64,3,768]{2,1,0:T(4,128)(2,1)}), bf16[64,3,768]{2,1,0:T(4,128)(2,1)}, u32[]{:S(2)}, u32[]{:S(2)}) async-start(bf16[64,3,768]{2,1,0:T(4,128)(2,1)} %reshape.761), calls=%async_computation.7 | async-start | bytes 786432 | tf_op jit(solution)/shard_map/all_to_all | solution.py:230
  455.8 104.9 %reduce-scatter.16.cloned.1.call-start = ((), (), s32[]{:S(2)}) async-start(), calls=%async_computation.24 | async-start | bytes 3342336
  485.4 77.1 %copy-start.105 = (f32[64]{0:T(128)S(1)}, f32[64]{0:T(128)}, u32[]{:S(2)}) copy-start(f32[64]{0:T(128)} %copy-done.104) | copy-start | bytes 772
  566.4 3.2 collective-permute-start.2
  605.8 16.7 %all-to-all-start.9 = ((bf16[64,3,768]{2,1,0:T(4,128)(2,1)}), bf16[64,3,768]{2,1,0:T(4,128)(2,1)}, u32[]{:S(2)}, u32[]{:S(2)}) async-start(bf16[64,3,768]{2,1,0:T(4,128)(2,1)} %reshape.769), calls=%async_computation.9 | async-start | bytes 786432 | tf_op jit(solution)/shard_map/all_to_all | solution.py:230
  616.7 105.0 %reduce-scatter.18.cloned.1.call-start = ((), (), s32[]{:S(2)}) async-start(), calls=%async_computation.25 | async-start | bytes 3342336
  646.4 77.2 %copy-start.102 = (f32[64]{0:T(128)S(1)}, f32[64]{0:T(128)}, u32[]{:S(2)}) copy-start(f32[64]{0:T(128)} %copy-done.101) | copy-start | bytes 772
  727.4 3.2 collective-permute-start.3
  766.8 16.7 %all-to-all-start.11 = ((bf16[64,3,768]{2,1,0:T(4,128)(2,1)}), bf16[64,3,768]{2,1,0:T(4,128)(2,1)}, u32[]{:S(2)}, u32[]{:S(2)}) async-start(bf16[64,3,768]{2,1,0:T(4,128)(2,1)} %reshape.777), calls=%async_computation.11 | async-start | bytes 786432 | tf_op jit(solution)/shard_map/all_to_all | solution.py:230
  777.7 104.9 %reduce-scatter.20.cloned.1.call-start = ((), (), s32[]{:S(2)}) async-start(), calls=%async_computation.26 | async-start | bytes 3342336
  807.4 246.1 %reduce-scatter.14.cloned.1.call-start = ((), (), s32[]{:S(2)}) async-start(), calls=%async_computation.21 | async-start | bytes 1253376 | tf_op jit(solution)/shard_map/reduce_scatter | solution.py:310
  811.0 242.5 %reduce-scatter.12.cloned.1.call-start = ((), (), s32[]{:S(2)}) async-start(), calls=%async_computation.20 | async-start | bytes 3760128 | tf_op jit(solution)/shard_map/reduce_scatter | solution.py:307
  821.8 62.7 %copy-start.111 = (f32[64]{0:T(128)S(1)}, f32[64]{0:T(128)}, u32[]{:S(2)}) copy-start(f32[64]{0:T(128)} %copy-done.110) | copy-start | bytes 772
  899.9 23.2 %all-to-all-start.5 = ((bf16[64,3,768]{2,1,0:T(4,128)(2,1)}), bf16[64,3,768]{2,1,0:T(4,128)(2,1)}, u32[]{:S(2)}, u32[]{:S(2)}) async-start(bf16[64,3,768]{2,1,0:T(4,128)(2,1)} %reshape.757), calls=%async_computation.5 | async-start | bytes 786432 | tf_op jit(solution)/shard_map/all_to_all | solution.py:146
  910.4 191.6 %all-reduce.11.cloned.1.call-start = ((), (), s32[]{:S(2)}) async-start(), calls=%async_computation.27 | async-start | bytes 589824 | tf_op jit(solution)/shard_map/psum | solution.py:324
  (134 other events, 767.0 us)
Sparse Core Ops, SparseCore 0:
  10.2 48.1 all-gather.16
  62.1 47.0 all-gather.10
  111.3 42.3 all-gather.18
  212.2 46.9 all-gather.12
  338.4 50.7 all-gather.14
  485.6 75.0 reduce-scatter.15
  646.5 75.1 reduce-scatter.17
  807.5 75.0 reduce-scatter.19
  885.9 74.6 reduce-scatter.13
  963.8 75.9 reduce-scatter.11
  1053.7 48.2 all-reduce.10
where the time goes:
time: 1130 us; the launch traced here: 1110 us
  waiting for transfers between devices  411 us (36%)
  blocking collectives  226 us (20%)
  matrix products  220 us (19%)
  local copies, waits for them, and re-layouts  137 us (12%)
  starting transfers between devices  71.1 us (6%)
  other arithmetic  29.9 us (3%)
  between operations  17.7 us (2%)
    unnamed x14, waiting for transfers between devices  205 us
    unnamed x2, blocking collectives  94.4 us
    all_gather x3, waiting for transfers between devices, body(): lax.all_gather(query_key_value[:, model_width:], 'shard', axis=0, tiled=T...  91.5 us
    unnamed x288, local copies, waits for them, and re-layouts  55.5 us
    psum x1, waiting for transfers between devices, body(): lax.psum(shares[0].astype(jnp.bfloat16), 'replica').astype(jnp.float32)  45.5 us
    all_to_all x2, blocking collectives, body(): lax.all_to_all(grad_slots, ('shard', 'replica'), split_axis=0, concat_axi...  34.4 us
    all_to_all x2, blocking collectives, body(): lax.all_to_all(result, ('shard', 'replica'), split_axis=0, concat_axis=0,...  33.5 us
    all_to_all x2, blocking collectives, body(): lax.all_to_all(outgoing, ('shard', 'replica'), split_axis=0, concat_axis=...  32.9 us
  transfers between devices with their start and end apart: 21, of which 17 were waited for; matrix products, arithmetic and copies ran while one was open for 15% of the time, Pallas kernels for 0%

commit v1 on v0

v1 whole, which is shorter than its diff:
```python
import jax
import jax.numpy as jnp
from jax import lax
from jax.experimental import pallas as pl
from jax.experimental.pallas import tpu as pltpu
from jax.sharding import PartitionSpec as P

MESH = pl.DeviceIdType.MESH
F32 = jnp.float32
BF16 = jnp.bfloat16
HIGH = lax.Precision.HIGHEST

D, HEADS, HD, FF = 768, 12, 64, 3072
LENGTH, ROWS, EXPERTS, SLOTS = 1024, 64, 64, 8
SHARDS, REPLICAS = 16, 4
TOK = 2 * ROWS
SLOT_ROWS = EXPERTS * SLOTS
BAND = LENGTH + 128
TILE = 256
C0 = 0.7978845608028654
C1 = C0 * 0.044715

MISC, GA1, GB1, GA2, GB2 = 0, 1, 2, 3, 4
QKV, MIX, DOUT, DQKV = 6, 8, 10, 12
DISP, RET, DY, DEXP, XPASS, GPASS = 14, 15, 16, 17, 18, 19
GTAB, SMALL, GW, GX, SX = 20, 21, 22, 23, 24
WIN, WOUT, OWIN, OWOUT = 25, 26, 27, 28

SCRATCH = dict(
    ga=((4, 4, 48, 1536), BF16),
    gb=((4, 4, 48, 1536), BF16),
    mr=((32, 8, 128), F32),
    gains=((8, D), F32),
    tb=((2, 128, LENGTH), F32),
    gg=((128, BAND), F32),
    win=((D, FF), BF16),
    wout=((FF, D), BF16),
    qs=((24, 64, 256), BF16),
    qr=((2, 16, 64, 256), BF16),
    os=((2, 16, 64, 128), BF16),
    mx=((24, 64, 128), BF16),
    mixed=((TOK, D), BF16),
    nrm=((TOK, D), BF16),
    hidden=((TOK, D), F32),
    xsend=((TOK, D), BF16),
    xin=((TOK, D), BF16),
    gin=((TOK, D), BF16),
    ds=((EXPERTS, SLOTS, D), BF16),
    dr=((EXPERTS, SLOTS, D), BF16),
    rs=((EXPERTS, SLOTS, D), BF16),
    rr=((EXPERTS, SLOTS, D), BF16),
    ys=((EXPERTS, SLOTS, D), BF16),
    yr=((EXPERTS, SLOTS, D), BF16),
    es=((EXPERTS, SLOTS, D), BF16),
    er=((EXPERTS, SLOTS, D), BF16),
    rows=((SLOT_ROWS, D), BF16),
    dyrows=((SLOT_ROWS, D), BF16),
    act=((SLOT_ROWS, FF), BF16),
    dg=((SLOT_ROWS, FF), BF16),
    acc=((SLOT_ROWS, D), F32),
    lse=((2, LENGTH, 1), F32),
    dos=((24, 64, 128), BF16),
    dor=((2, 16, 64, 128), BF16),
    dks=((2, 16, 64, 256), BF16),
    dkr=((24, 64, 256), BF16),
    dkv=((LENGTH, 128), F32),
    dqk=((TOK, 1536), BF16),
    dvv=((TOK, D), BF16),
    dh=((TOK, D), F32),
    gp=((16, 48, 3072), BF16),
    gr=((16, 48, 3072), BF16),
    gxs=((48, 3072), BF16),
    gx=((4, 48, 3072), BF16),
    sm=((8, D), F32),
    smr=((16, 8, D), F32),
    sxs=((8, D), F32),
    sx=((4, 8, D), F32),
    gts=((2, 8, 128), F32),
    gtr=((24, 8, 128), F32),
)
INPUTS = ("tok", "cot", "wcat", "misc", "oh", "segr", "segc", "smat", "stmat", "gh", "gl", "gth", "gtl", "winh", "wouth")
OUTPUTS = ("acts", "sgr", "gwo", "smo", "gwin", "gwout")


def dot(a, b, **kw):
    return jnp.dot(a, b, preferred_element_type=F32, **kw)


def dot_nt(a, b, **kw):
    return lax.dot_general(a, b, (((1,), (1,)), ((), ())), preferred_element_type=F32, **kw)


def dot_tn(a, b, **kw):
    return lax.dot_general(a, b, (((0,), (0,)), ((), ())), preferred_element_type=F32, **kw)


def loop(count, step):
    def wrapped(i, carry):
        step(i)
        return carry
    lax.fori_loop(0, count, wrapped, 0)


def kernel(*refs):
    names = INPUTS + OUTPUTS + tuple(SCRATCH) + ("ssem", "rsem")
    R = dict(zip(names, refs))
    ssem, rsem = R["ssem"], R["rsem"]
    c = lax.axis_index("section")
    s = lax.axis_index("shard")
    r = lax.axis_index("replica")
    e = s * REPLICAS + r
    y = s // 4
    z = s % 4

    def push(src, dst, i, tc, ts, tr):
        same = (tc == c) & (ts == s) & (tr == r)

        @pl.when(same)
        def _():
            pltpu.make_async_copy(src, dst, rsem.at[i]).start()

        @pl.when(jnp.logical_not(same))
        def _():
            send(src, dst, i, tc, ts, tr)

    def send(src, dst, i, tc, ts, tr):
        pltpu.make_async_remote_copy(
            src_ref=src, dst_ref=dst, send_sem=ssem.at[i], recv_sem=rsem.at[i],
            device_id=(tc, ts, tr), device_id_type=MESH,
        ).start()

    def got(ref, i):
        pltpu.make_async_copy(ref, ref, rsem.at[i]).wait()

    def sent(ref, i):
        pltpu.make_async_copy(ref, ref, ssem.at[i]).wait()

    pltpu.make_async_copy(R["winh"], R["win"], rsem.at[WIN]).start()
    pltpu.make_async_copy(R["wouth"], R["wout"], rsem.at[WOUT]).start()

    def misc_step(i):
        push(R["misc"], R["mr"].at[c * 16 + s], MISC, i // 16, i % 16, r)
    loop(32, misc_step)

    wcat, ga, gb = R["wcat"], R["ga"], R["gb"]

    def gather_one(i):
        push(wcat.at[:, pl.ds(0, 1536)], ga.at[y, z], GA1, c, y * 4 + i, r)
        push(wcat.at[:, pl.ds(1536, 1536)], gb.at[y, z], GB1, c, i * 4 + z, r)
    loop(4, gather_one)
    got(ga.at[y], GA1)
    got(gb.at[:, z], GB1)

    def gather_two(i):
        @pl.when(i != y)
        def _():
            send(ga.at[y], ga.at[y], GA2, c, i * 4 + z, r)

        @pl.when(i != z)
        def _():
            send(gb.at[:, z], gb.at[:, z], GB2, c, y * 4 + i, r)
    loop(4, gather_two)

    got(R["mr"], MISC)
    mr = R["mr"]
    lane = lax.broadcasted_iota(jnp.int32, (8, D), 1)
    total = jnp.zeros((8, D), F32)
    for k in range(SHARDS):
        piece = jnp.concatenate([mr[c * 16 + k], jnp.zeros((8, D - 128), F32)], axis=1)
        piece = jnp.where(lane < 48, piece, 0.0)
        total = total + (pltpu.roll(piece, 48 * k, 1) if k else piece)
    R["gains"][...] = total

    is_head = s < HEADS

    @pl.when(is_head)
    def _():
        sub = lax.broadcasted_iota(jnp.int32, (8, 128), 0)
        for l in range(2):
            tab = jnp.zeros((8, 128), F32)
            for k in range(SHARDS):
                tab = tab + (pltpu.roll(mr[l * 16 + k], 2 * k, 1) if k else mr[l * 16 + k])
            tab = jnp.where(sub == 2 + s // 2, tab, 0.0)
            tab = pltpu.roll(tab, (s % 2) * 64, 1)
            row = jnp.sum(tab, axis=0, keepdims=True)
            base = dot(jnp.broadcast_to(row, (8, 128)).astype(BF16), R["oh"][...])
            band = jnp.broadcast_to(base[0:1], (128, BAND))
            band = pltpu.roll(band, BAND - 127, 1, stride=1, stride_axis=0)
            R["tb"][l] = band[:, :LENGTH]

    got(ga.at[pl.ds(0, 3)], GA2)
    got(gb.at[pl.ds(0, 3)], GB2)

    def head_parts(l):
        both = R["qr"][l].reshape(LENGTH, 256)
        return both[:, 0:64], both[:, 64:128], both[:, 128:192] * BF16(0.125)

    def logits(l, b, q, keys):
        nk = 128 * (b + 1)
        scores = dot_nt(q[128 * b:nk], keys[:nk]) + R["tb"][l, :, 896 - 128 * b:1024]
        row = lax.broadcasted_iota(jnp.int32, (128, nk), 0) + 128 * b
        col = lax.broadcasted_iota(jnp.int32, (128, nk), 1)
        ok = (col <= row) & (R["segc"][128 * b:nk, :] == R["segr"][:, :nk])
        return jnp.where(ok, scores, -1e30)

    def head_fwd(l):
        got(R["qr"].at[l], QKV + l)
        keys, values, q = head_parts(l)
        for b in range(8):
            nk = 128 * (b + 1)
            lg = logits(l, b, q, keys)
            top = jnp.max(lg, axis=1, keepdims=True)
            ex = jnp.exp(lg - top)
            tot = jnp.sum(ex, axis=1, keepdims=True)
            out = dot(ex.astype(BF16), values[:nk]) / tot
            R["os"][l, 2 * b:2 * b + 2, :, 0:64] = out.astype(BF16).reshape(2, 64, 64)
            R["lse"][l, 128 * b:nk, :] = top + jnp.log(tot)

        def back(i):
            push(R["os"].at[l, i], R["mx"].at[c * HEADS + s], MIX + l, l, i, r)
        loop(SHARDS, back)

    def head_bwd(l):
        got(R["dor"].at[l], DOUT + l)
        keys, values, q = head_parts(l)
        dor, dks, dkv, gg = R["dor"], R["dks"], R["dkv"], R["gg"]
        dkv[...] = jnp.zeros(dkv.shape, F32)
        gg[...] = jnp.zeros(gg.shape, F32)
        for b in range(8):
            nk = 128 * (b + 1)
            qb = q[128 * b:nk]
            prob = jnp.exp(logits(l, b, q, keys) - R["lse"][l, 128 * b:nk, :])
            do = dor[l, 2 * b:2 * b + 2, :, 0:64].reshape(128, 64)
            dp = dot_nt(do, values[:nk])
            delta = jnp.sum(prob * dp, axis=1, keepdims=True)
            dlog = prob * (dp - delta)
            gg[:, 896 - 128 * b:1024] += dlog
            low = dlog.astype(BF16)
            dq = dot(low, keys[:nk]) * 0.125
            dks[l, 2 * b:2 * b + 2, :, 128:192] = dq.astype(BF16).reshape(2, 64, 64)
            dkv[:nk, 0:64] += dot_tn(low, qb)
            dkv[:nk, 64:128] += dot_tn(prob.astype(BF16), do)
        dks[l, :, :, 0:128] = dkv[...].astype(BF16).reshape(16, 64, 128)

        def back(i):
            push(dks.at[l, i], R["dkr"].at[c * HEADS + s], DQKV + l, l, i, r)
        loop(SHARDS, back)
        flip = (lax.broadcasted_iota(jnp.int32, (128, 128), 0) + lax.broadcasted_iota(jnp.int32, (128, 128), 1)) == 127
        band = dot(flip.astype(F32), gg[...], precision=HIGH)
        band = pltpu.roll(band, 0, 1, stride=1, stride_axis=0)
        diag = jnp.sum(band, axis=0, keepdims=True)
        tg = dot_nt(jnp.broadcast_to(diag, (8, BAND)), R["oh"][...].astype(F32), precision=HIGH)
        sub = lax.broadcasted_iota(jnp.int32, (8, 128), 0)
        tg = jnp.where(sub == 2 + s // 2, pltpu.roll(tg, (s % 2) * 64, 1), 0.0)
        R["gts"][l] = tg

        def back_table(i):
            push(R["gts"].at[l], R["gtr"].at[c * HEADS + s], GTAB, l, i, r)
        loop(SHARDS, back_table)

    def norm(x):
        return x * lax.rsqrt(jnp.mean(x * x, axis=1, keepdims=True) + 1e-06)

    def norm_back(x, gain, dn):
        rstd = lax.rsqrt(jnp.mean(x * x, axis=1, keepdims=True) + 1e-06)
        n = x * rstd
        dgain = jnp.sum(dn * n, axis=0, keepdims=True)
        dng = dn * gain
        return rstd * (dng - n * jnp.mean(dng * n, axis=1, keepdims=True)), dgain

    def spread(buf, dst, i, l):
        def step(k):
            push(buf.at[k], dst.at[e], i, l, k // REPLICAS, k % REPLICAS)
        loop(EXPERTS, step)

    def slots(value):
        return value.reshape(EXPERTS, SLOTS, D).astype(BF16)

    def flat(ref):
        return ref[...].astype(F32).reshape(SLOT_ROWS, D).astype(BF16)

    def to_heads(buf, dst, i):
        def step(u):
            push(buf.at[u], dst.at[s], i, u // HEADS, u % HEADS, r)
        loop(24, step)

    def tile(t):
        return pl.ds(pl.multiple_of(t * TILE, TILE), TILE)

    def layer_in(l):
        return R["tok"][...] if l == 0 else R["xin"][...]

    def wk():
        return ga[...].reshape(D, 1536)

    def wv():
        return gb[:, :, :, 0:D].reshape(D, D)

    def wo():
        return gb[:, :, :, D:2 * D].reshape(D, D)

    def fwd_one(l):
        if l == 1:
            got(R["xin"], XPASS)
        x = layer_in(l).astype(F32)
        nrm = (norm(x) * R["gains"][0:1, :]).astype(BF16)
        R["nrm"][...] = nrm
        qk = dot(nrm, wk()).astype(BF16)
        v = dot(nrm, wv()).astype(BF16)
        qs = R["qs"]
        for u in range(24):
            rows = slice(64 * (u // HEADS), 64 * (u // HEADS) + 64)
            h = 64 * (u % HEADS)
            qs[u, :, 0:64] = qk[rows, D + h:D + h + 64]
            qs[u, :, 64:128] = v[rows, h:h + 64]
            qs[u, :, 128:192] = qk[rows, h:h + 64]
        to_heads(qs, R["qr"].at[l], QKV + l)

    def fwd_two(l):
        got(R["mx"], MIX + l)
        mx, mixed = R["mx"], R["mixed"]
        for u in range(24):
            rows = slice(64 * (u // HEADS), 64 * (u // HEADS) + 64)
            h = 64 * (u % HEADS)
            mixed[rows, h:h + 64] = mx[u, :, 0:64]
        hidden = layer_in(l).astype(F32) + dot(mixed[...], wo())
        R["hidden"][...] = hidden
        nrm2 = (norm(hidden) * R["gains"][1:2, :]).astype(BF16)
        R["ds"][...] = slots(dot(R["smat"][...], nrm2))
        spread(R["ds"], R["dr"], DISP, l)

        got(R["win"], WIN)
        got(R["wout"], WOUT)
        got(R["dr"], DISP)
        rows, acc, win, wout = R["rows"], R["acc"], R["win"], R["wout"]
        rows[...] = flat(R["dr"])
        acc[...] = jnp.zeros(acc.shape, F32)

        def ffn(t):
            at = tile(t)
            pre = dot(rows[...], win[:, at])
            sq = pre * pre
            th = jnp.tanh(pre * (C0 + C1 * sq))
            half = 0.5 * (1.0 + th)
            act = (pre * half).astype(BF16)
            R["act"][:, at] = act
            R["dg"][:, at] = (half + 0.5 * pre * (1.0 - th * th) * (C0 + 3.0 * C1 * sq)).astype(BF16)
            acc[...] += dot(act, wout[at, :])
        loop(FF // TILE, ffn)
        R["rs"][...] = slots(acc[...])
        spread(R["rs"], R["rr"], RET, l)
        got(R["rr"], RET)
        back = flat(R["rr"])
        out = R["hidden"][...] + dot(R["gth"][...], back) + dot(R["gtl"][...], back)
        R["acts"][...] = out.astype(BF16)
        if l == 0:
            R["xsend"][...] = out.astype(BF16)
            send(R["xsend"], R["xin"], XPASS, 1, s, r)

    def bwd_one(l):
        if l == 0:
            got(R["gin"], GPASS)
        g = R["cot"][...] if l == 1 else R["gin"][...]
        R["ys"][...] = slots(dot(R["gh"][...], g) + dot(R["gl"][...], g))
        spread(R["ys"], R["yr"], DY, l)
        got(R["yr"], DY)
        rows, acc, win, wout, act, dg, dyrows = (R[k] for k in ("rows", "acc", "win", "wout", "act", "dg", "dyrows"))
        dyrows[...] = flat(R["yr"])
        acc[...] = jnp.zeros(acc.shape, F32)

        def ffn(t):
            at = tile(t)
            dact = dot_nt(dyrows[...], wout[at, :])
            dpre = (dact * dg[:, at].astype(F32)).astype(BF16)
            dg[:, at] = dpre
            acc[...] += dot_nt(dpre, win[:, at])
        loop(FF // TILE, ffn)
        R["es"][...] = slots(acc[...])
        spread(R["es"], R["er"], DEXP, l)

        def weights(t):
            at = tile(t)
            win[:, at] = dot_tn(rows[...], dg[:, at]).astype(BF16)
            wout[at, :] = dot_tn(act[:, at], dyrows[...]).astype(BF16)
        loop(FF // TILE, weights)
        pltpu.make_async_copy(win, R["gwin"], rsem.at[OWIN]).start()
        pltpu.make_async_copy(wout, R["gwout"], rsem.at[OWOUT]).start()

        got(R["er"], DEXP)
        dn2 = dot(R["stmat"][...], flat(R["er"]))
        dx, dgain = norm_back(R["hidden"][...], R["gains"][1:2, :], dn2)
        R["sm"][...] = jnp.zeros((8, D), F32)
        R["sm"][1:2, :] = dgain
        dh = g.astype(F32) + dx
        R["dh"][...] = dh
        dattn = dh.astype(BF16)
        dmix = dot_nt(dattn, wo()).astype(BF16)
        dos = R["dos"]
        for u in range(24):
            rs = slice(64 * (u // HEADS), 64 * (u // HEADS) + 64)
            h = 64 * (u % HEADS)
            dos[u, :, 0:64] = dmix[rs, h:h + 64]
        to_heads(dos, R["dor"].at[l], DOUT + l)
        gout = dot_tn(R["mixed"][...], dattn)
        R["gp"][:, :, 2304:3072] = gout.astype(BF16).reshape(16, 48, D)

    def bwd_two(l):
        got(R["dkr"], DQKV + l)
        dkr, dqk, dvv, gp = R["dkr"], R["dqk"], R["dvv"], R["gp"]
        for u in range(24):
            rs = slice(64 * (u // HEADS), 64 * (u // HEADS) + 64)
            h = 64 * (u % HEADS)
            dqk[rs, D + h:D + h + 64] = dkr[u, :, 0:64]
            dvv[rs, h:h + 64] = dkr[u, :, 64:128]
            dqk[rs, h:h + 64] = dkr[u, :, 128:192]
        dn = dot_nt(dqk[...], wk()) + dot_nt(dvv[...], wv())
        dx, dgain = norm_back(layer_in(l).astype(F32), R["gains"][0:1, :], dn)
        low = (R["dh"][...] + dx).astype(BF16)
        R["sgr"][...] = low
        if l == 1:
            R["xsend"][...] = low
            send(R["xsend"], R["gin"], GPASS, 0, s, r)
        R["sm"][0:1, :] = dgain
        nrm = R["nrm"]
        for t in range(6):
            gp[:, :, 256 * t:256 * t + 256] = dot_tn(nrm[...], dqk[:, 256 * t:256 * t + 256]).astype(BF16).reshape(16, 48, 256)
        for t in range(3):
            gp[:, :, 1536 + 256 * t:1792 + 256 * t] = dot_tn(nrm[...], dvv[:, 256 * t:256 * t + 256]).astype(BF16).reshape(16, 48, 256)

        def reduce(i):
            push(gp.at[i], R["gr"].at[s], GW, l, i, r)
            push(R["sm"], R["smr"].at[s], SMALL, l, i, r)
        loop(SHARDS, reduce)

    for l in range(2):
        pl.when(c == l)(lambda l=l: fwd_one(l))
        pl.when(is_head)(lambda l=l: head_fwd(l))
        pl.when(c == l)(lambda l=l: fwd_two(l))
    for l in (1, 0):
        pl.when(c == l)(lambda l=l: bwd_one(l))
        pl.when(is_head)(lambda l=l: head_bwd(l))
        pl.when(c == l)(lambda l=l: bwd_two(l))

    got(R["gr"], GW)
    got(R["smr"], SMALL)
    got(R["gtr"], GTAB)
    gr, gx, sx = R["gr"], R["gx"], R["sx"]
    for t in range(12):
        cols = slice(256 * t, 256 * t + 256)
        part = gr[0, :, cols].astype(F32)
        for k in range(1, SHARDS):
            part = part + gr[k, :, cols].astype(F32)
        R["gxs"][:, cols] = part.astype(BF16)
    small = R["smr"][0]
    for k in range(1, SHARDS):
        small = small + R["smr"][k]
    table = R["gtr"][0]
    for k in range(1, 24):
        table = table + R["gtr"][k]
    R["sxs"][...] = small + jnp.concatenate([table, jnp.zeros((8, D - 128), F32)], axis=1)

    def over_replicas(i):
        push(R["gxs"], gx.at[r], GX, c, s, i)
        push(R["sxs"], sx.at[r], SX, c, s, i)
    loop(REPLICAS, over_replicas)
    got(gx, GX)
    got(sx, SX)
    R["gwo"][...] = (gx[0].astype(F32) + gx[1].astype(F32) + gx[2].astype(F32) + gx[3].astype(F32)).astype(BF16)
    R["smo"][...] = sx[0] + sx[1] + sx[2] + sx[3]

    sent(mr.at[pl.ds(0, 31)], MISC)
    sent(ga.at[0, pl.ds(0, 3)], GA1)
    sent(gb.at[0, pl.ds(0, 3)], GB1)
    sent(ga.at[pl.ds(0, 3)], GA2)
    sent(gb.at[pl.ds(0, 3)], GB2)
    few = EXPERTS - 1
    sent(R["ds"].at[pl.ds(0, few)], DISP)
    sent(R["rs"].at[pl.ds(0, few)], RET)
    sent(R["ys"].at[pl.ds(0, few)], DY)
    sent(R["es"].at[pl.ds(0, few)], DEXP)
    sent(R["gp"].at[pl.ds(0, 15)], GW)
    sent(R["smr"].at[pl.ds(0, 15)], SMALL)
    sent(gx.at[pl.ds(0, 3)], GX)
    sent(sx.at[pl.ds(0, 3)], SX)
    got(R["win"], OWIN)
    got(R["wout"], OWOUT)
    for l in range(2):
        @pl.when(c == l)
        def _():
            sent(R["xsend"], XPASS if l == 0 else GPASS)
            for buf, i in ((R["qs"], QKV + l), (R["dos"], DOUT + l)):
                pl.when(is_head)(lambda buf=buf, i=i: sent(buf.at[pl.ds(0, 23)], i))
                pl.when(jnp.logical_not(is_head))(lambda buf=buf, i=i: sent(buf, i))

        @pl.when(is_head)
        def _():
            for buf, i in ((R["os"], MIX + l), (R["dks"], DQKV + l)):
                pl.when(c == l)(lambda buf=buf, i=i: sent(buf.at[l, pl.ds(0, 15)], i))
                pl.when(c != l)(lambda buf=buf, i=i: sent(buf.at[l], i))

    @pl.when(is_head)
    def _():
        sent(mr.at[pl.ds(0, 31)], GTAB)


def body(tokens, cotangent, wqkv, wout, gain_attn, gain_ffn, rel_table, w_in, w_out_exp, expert_ids, gates, seg_ids, buckets):
    shard = lax.axis_index("shard")
    wcat = jnp.concatenate([wqkv[0], wout[0]], axis=1)
    pad = lambda v, n: jnp.pad(v, ((0, 0), (0, n - v.shape[1])))
    table = rel_table[0].astype(F32).reshape(2, 6, 2).transpose(1, 2, 0)
    table = pad(table.reshape(12, 2), 64).reshape(6, 128)
    misc = jnp.concatenate([pad(gain_attn.astype(F32), 128), pad(gain_ffn.astype(F32), 128), table], axis=0)
    oh = (buckets[::-1][None, :] == jnp.arange(128)[:, None]).astype(BF16)
    oh = pad(oh, BAND)
    seg = lax.dynamic_index_in_dim(seg_ids, lax.axis_index("section"), 0, keepdims=False).astype(F32)
    ids = expert_ids[0].reshape(2, TOK)
    before = (jnp.arange(TOK)[:, None] > jnp.arange(TOK)[None, :])[None]
    rank = jnp.sum(((ids[:, :, None] == ids[:, None, :]) & before).astype(jnp.int32), axis=2)
    slot = (ids * SLOTS + jnp.arange(2)[:, None] * 3 + rank).reshape(TOK, 2)
    gate = gates[0].reshape(TOK, 2)
    every = jnp.arange(SLOT_ROWS)

    def matrices(hit_a, hit_b, gate_a, gate_b):
        full = jnp.where(hit_a, gate_a, 0.0) + jnp.where(hit_b, gate_b, 0.0)
        high = lax.reduce_precision(full, 8, 7)
        return (hit_a | hit_b).astype(BF16), high.astype(BF16), (full - high).astype(BF16)
    smat, gh, gl = matrices(slot[None, :, 0] == every[:, None], slot[None, :, 1] == every[:, None], gate[None, :, 0], gate[None, :, 1])
    stmat, gth, gtl = matrices(slot[:, 0:1] == every[None, :], slot[:, 1:2] == every[None, :], gate[:, 0:1], gate[:, 1:2])

    vmem = pl.BlockSpec(memory_space=pltpu.VMEM)
    hbm = pl.BlockSpec(memory_space=pl.ANY)
    out = jax.ShapeDtypeStruct
    acts, sgr, gwo, smo, gwin, gwout = pl.pallas_call(
        kernel,
        out_shape=(out((TOK, D), BF16), out((TOK, D), BF16), out((48, 3072), BF16), out((8, D), F32), out((D, FF), BF16), out((FF, D), BF16)),
        in_specs=[vmem] * 13 + [hbm] * 2,
        out_specs=(vmem, vmem, vmem, vmem, hbm, hbm),
        scratch_shapes=[pltpu.VMEM(*v) for v in SCRATCH.values()] + [pltpu.SemaphoreType.DMA((32,)), pltpu.SemaphoreType.DMA((32,))],
        compiler_params=pltpu.CompilerParams(has_side_effects=True, vmem_limit_bytes=64 * 1024 * 1024 - 65536),
        name="relay",
    )(tokens.reshape(TOK, D), cotangent.reshape(TOK, D), wcat, misc, oh, seg[None, :], seg[:, None],
      smat, stmat, gh, gl, gth, gtl, w_in[0, 0], w_out_exp[0, 0])
    gains = lax.dynamic_slice(smo, (0, shard * 48), (2, 48)).astype(BF16)
    grad_table = smo[2:8, 0:128].reshape(HEADS, 64)[:, 0:32].T
    grad_table = lax.dynamic_slice(grad_table, (shard * 2, 0), (2, HEADS)).astype(BF16)
    return (
        acts.reshape(1, 2, ROWS, D),
        sgr.reshape(1, 2, ROWS, D),
        gwo[None, :, 0:2304],
        gwo[None, :, 2304:3072],
        gains[0:1],
        gains[1:2],
        grad_table[None],
        gwin[None, None],
        gwout[None, None],
    )


def solution(mesh):
    in_specs = (
        P("replica", "shard", None),
        P("replica", "shard", None),
        P("section", "shard", None),
        P("section", "shard", None),
        P("section", "shard"),
        P("section", "shard"),
        P("section", "shard", None),
        P("section", ("shard", "replica"), None, None),
        P("section", ("shard", "replica"), None, None),
        P("section", "replica", "shard", None),
        P("section", "replica", "shard", None),
        P("replica", None),
        P(),
    )
    out_specs = (
        P("section", "replica", "shard", None),
        P("section", "replica", "shard", None),
        P("section", "shard", None),
        P("section", "shard", None),
        P("section", "shard"),
        P("section", "shard"),
        P("section", "shard", None),
        P("section", ("shard", "replica"), None, None),
        P("section", ("shard", "replica"), None, None),
    )
    return jax.shard_map(body, mesh=mesh, in_specs=in_specs, out_specs=out_specs, check_vma=False)
```

time: 1130 us -> 395 us (0.35); the launches traced: 1110 us -> 395 us
  waiting for transfers between devices: 411 us -> 0 us
  Pallas kernels: 0 us -> 363 us
  blocking collectives: 226 us -> 0 us
  matrix products: 220 us -> 0 us
  local copies, waits for them, and re-layouts: 137 us -> 21.3 us
  starting transfers between devices: 71.1 us -> 0 us
  other arithmetic: 29.9 us -> 9.81 us
  between operations: 17.7 us -> 0.73 us
    pallas_call x0 -> x1, Pallas kernels: none -> 363 us  [body(): pl.pallas_call(kernel, out_shape=(out((TOK, D), BF16), out((TOK, D), BF16...]
    dot_general x70 -> x0, matrix products: 220 us -> none  [the longest x3 20.4 us: body(): jnp.einsum('zxo,gxo->gz', score_gradient, local_indicator_matrix, precisi...]
    unnamed x14 -> x0, waiting for transfers between devices: 205 us -> none
    all_gather x5 -> x0, waiting for transfers between devices: 137 us -> none  [the longest x3 91.5 us: body(): lax.all_gather(query_key_value[:, model_width:], 'shard', axis=0, tiled=T...]
    all_to_all x6 -> x0, blocking collectives: 101 us -> none  [the longest x2 34.4 us: body(): lax.all_to_all(grad_slots, ('shard', 'replica'), split_axis=0, concat_axi...]
    unnamed x2 -> x0, blocking collectives: 94.4 us -> none
    all_to_all x6 -> x0, starting transfers between devices: 64.7 us -> none  [the longest x3 32.8 us: body(): lax.all_to_all(grad_rows, ('shard', 'replica'), split_axis=0, concat_axis...]
    reshape x30 -> x3, local copies, waits for them, and re-layouts: 50.9 us -> 0.26 us  [the longest x2 0.17 us: body(): table = pad(table.reshape(12, 2), 64).reshape(6, 128)]
  transfers between devices with their start and end apart: 21 -> 0, of which waited for: 17 -> 0; matrix products, arithmetic and copies ran while one was open for 15% -> 0% of each run, Pallas kernels for 0% -> 0%
where the time goes in v1:
time: 395 us
  Pallas kernels  363 us (92%)
  local copies, waits for them, and re-layouts  21.3 us (5%)
  other arithmetic  9.81 us (2%)
    pallas_call x1, Pallas kernels, body(): pl.pallas_call(kernel, out_shape=(out((TOK, D), BF16), out((TOK, D), BF16...  363 us
    unnamed x12, local copies, waits for them, and re-layouts  12.6 us

profile of v1, /device:TPU:116, one launch (start us, length us, event | category | flops | bytes accessed | tf_op | source)
XLA Modules:
  0.0 395.0 jit_solution(10772415990508435030)
XLA Ops:
  0.8 0.7 copy.35
  1.6 0.7 broadcast_multiply_fusion
  2.4 0.7 convert_element_type.59
  3.4 1.3 fusion.11.refs_3_
  4.7 0.8 rev.3
  5.4 0.7 fusion.13
  6.1 1.3 dynamic-slice_convert_fusion.1.refs_5_
  7.4 0.8 copy.33
  8.9 0.8 fusion.5.refs_8_
  9.7 0.7 fusion.4.refs_7_
  10.4 0.7 pad_convert_fusion.refs_4_
  11.1 0.9 fusion.1
  12.0 0.8 fusion
  12.7 1.7 pad_maximum_fusion.refs_2_
  14.5 1.0 copy.36.refs_6_
  15.5 363.1 %relay.1 = (bf16[128,768]{1,0:T(8,128)(2,1)}, bf16[128,768]{1,0:T(8,128)(2,1)}, bf16[48,3072]{1,0:T(8,128)(2,1)}, f32[8,768]{1,0:T(8,128)}, bf16[768,3072]{1,0:T(8,128)(2,1)}, /*index=5*/bf16[3072,768]{1,0:T(8,128)(2,1)}) custom-call(bf16[128,768]{1,0:T(8,128)(2,1)} %bitcast.46, bf16[128,768]{1,0:T(8,128)(2,1)} %bitcast.47, ...), custom_call_target="tpu_custom_call" | custom-call | tf_op jit(solution)/shard_map/relay/pallas_call | solution.py:533
  378.6 0.8 dynamic-slice_convert_fusion.2
  379.9 0.7 slice.42
  381.3 1.5 slice_bitcast_fusion.1
  382.8 1.6 slice_bitcast_fusion
  384.5 1.6 copy.46
  386.1 1.8 copy.47
  387.9 4.9 %copy.48 = bf16[1,1,768,3072]{3,2,1,0:T(8,128)(2,1)} copy(bf16[1,1,768,3072]{3,2,1,0:T(8,128)(2,1)} %bitcast.42) | data formatting | bytes 9437184
  392.8 2.2 copy.49
  (28 shorter events, 2.6 us)
Async XLA Ops:
  386.1 6.7 %slice-start = ((s8[4718592]{0:T(1024)(128)(4,1)}), s8[4194304]{0:T(1024)(128)(4,1)S(1)}, s32[]{:S(2)}) async-start(s8[4718592]{0:T(1024)(128)(4,1)} %bitcast.39), calls=%async_computation | async-start | bytes 8388608
  387.9 4.9 %slice-start.1 = ((s8[4718592]{0:T(1024)(128)(4,1)}), s8[524288]{0:T(1024)(128)(4,1)S(1)}, s32[]{:S(2)}) async-start(s8[4718592]{0:T(1024)(128)(4,1)} %bitcast.39), calls=%async_computation.1 | async-start | bytes 1048576
